TPU v7x, 32 devices: a whole 2x2x4 slice. The times are simulated.
32 devices in a mesh: parts: 2 (over y), req: 4 (over z), tp: 4 (over x, core).
Axes of the slice: x: 2, y: 2, z: 4, core: 2. Of those that a mesh axis runs over, the one named last changes fastest.
Arguments:
- prompts: bfloat16 [8192, 8192], P(('parts', 'req'), 'tp'), parts along dimension 0, may hold values from -6 to 6
- kv_weight: bfloat16 [8192, 2048], P('tp', 'req'), may hold values from -0.0625 to 0.0625
- owners: int32 [8, 4], P(('parts', 'req')), parts along dimension 0, may hold values from 0 to 3, as said below
- pages: int32 [8, 4], P(('parts', 'req')), parts along dimension 0, may hold values from 1 to 40, as said below
- lengths: int32 [8, 4], P(('parts', 'req')), parts along dimension 0, may hold values from 1 to 640, as said below
- queries: bfloat16 [2, 32, 8192], P(None, ('parts', 'req'), 'tp'), parts along dimension 1, may hold values from -100 to 100
- new_kv: bfloat16 [2, 32, 2048], P(None, ('parts', 'req'), 'tp'), parts along dimension 1, may hold values from -100 to 100
Outputs:
- attended: bfloat16 [2, 32, 8192], P(None, ('parts', 'req'), 'tp'), parts along dimension 1
There are 2 independent parts, one for each index of `parts`. A program takes and returns all parts, laid end to end along the dimension named above; an argument that names none is the same for every part. Nothing has to cross between parts.
Inputs may be any that keep to these rules, and one draw needn't show every extreme that they name: Each row of owners names every decode owner once. Each row sums to 64; in each row one request has exactly 40 pages. lengths[o, g] is the token count of the request of group g served by owner o: more than 16 * (its pages - 1) and at most 16 * its pages.
All inputs are finite; a program needn't handle non-finite values.
Results may differ from a plain program's by a relative error of at most 0.017.
Values may be sent and summed in bfloat16 or wider, within the bound.
A program may use at most 64 MiB of HBM per device.

v0:
```python
import jax
import jax.numpy as jnp
from jax import lax
from jax.sharding import PartitionSpec as P

HD = 128
PAGE = 16
GQA = 8


def attend(queries, new_kv, cache, row_lengths):
    steps_count, rows_count = (queries.shape[0], queries.shape[1])
    heads_kv = new_kv.shape[2] // (2 * HD)
    slot_tokens = cache.shape[1]
    score_scale = HD ** (-0.5)
    asked = queries.reshape(steps_count, rows_count, heads_kv, GQA, HD)
    fresh = new_kv.reshape(steps_count, rows_count, heads_kv, 2, HD)
    stored = cache.reshape(rows_count, slot_tokens, heads_kv, 2, HD)
    cached = (
        jnp.einsum(
            "srhgd,rthd->srhgt", asked, stored[:, :, :, 0], preferred_element_type=jnp.float32
        )
        * score_scale
    )
    newer = (
        jnp.einsum(
            "srhgd,urhd->srhgu", asked, fresh[:, :, :, 0], preferred_element_type=jnp.float32
        )
        * score_scale
    )
    valid = jnp.arange(slot_tokens, dtype=jnp.int32)[None, :] < row_lengths[:, None]
    seen = jnp.arange(steps_count)[None, :] <= jnp.arange(steps_count)[:, None]
    cached = jnp.where(valid[None, :, None, None, :], cached, -1e30)
    newer = jnp.where(seen[:, None, None, None, :], newer, -1e30)
    top = jnp.maximum(jnp.max(cached, axis=-1), jnp.max(newer, axis=-1))[..., None]
    weight_cached = jnp.exp(cached - top)
    weight_newer = jnp.exp(newer - top)
    total = jnp.sum(weight_cached, axis=-1, keepdims=True) + jnp.sum(
        weight_newer, axis=-1, keepdims=True
    )
    prob_cached = (weight_cached / total).astype(jnp.bfloat16)
    prob_newer = (weight_newer / total).astype(jnp.bfloat16)
    mixed = jnp.einsum(
        "srhgt,rthd->srhgd", prob_cached, stored[:, :, :, 1], preferred_element_type=jnp.float32
    )
    mixed = mixed + jnp.einsum(
        "srhgu,urhd->srhgd", prob_newer, fresh[:, :, :, 1], preferred_element_type=jnp.float32
    )
    return mixed.astype(jnp.bfloat16).reshape(steps_count, rows_count, heads_kv * GQA * HD)


def on_device(prompts, kv_weight, owners, pages, lengths, queries, new_kv):
    owner_count = lax.axis_size("req")
    tokens_here = prompts.shape[0]
    group_pages = tokens_here // PAGE
    most_pages = 5 * group_pages // (2 * owner_count)
    slot_tokens = most_pages * PAGE
    partial_value = jnp.dot(
        prompts,
        lax.all_gather(kv_weight, "req", axis=1, tiled=True),
        preferred_element_type=jnp.float32,
    )
    key_value = lax.psum_scatter(
        partial_value.astype(jnp.bfloat16), "tp", scatter_dimension=1, tiled=True
    )
    width_here = key_value.shape[1]
    padded = jnp.concatenate(
        [key_value, jnp.zeros((slot_tokens, width_here), jnp.bfloat16)], axis=0
    )
    starts = jnp.cumsum(pages[0]) - pages[0]
    chosen_mask = (owners[0][None, :] == jnp.arange(owner_count, dtype=jnp.int32)[:, None]).astype(
        jnp.int32
    )
    target_starts = jnp.sum(chosen_mask * starts[None, :], axis=1) * PAGE
    outgoing = jax.vmap(lambda offset: lax.dynamic_slice_in_dim(padded, offset, slot_tokens, 0))(
        target_starts
    )
    incoming = lax.all_to_all(outgoing, "req", split_axis=0, concat_axis=0, tiled=True)
    return attend(queries, new_kv, incoming, lengths[0])


def solution(mesh):
    return jax.shard_map(
        on_device,
        mesh=mesh,
        in_specs=(
            P(("parts", "req"), "tp"),
            P("tp", "req"),
            P(("parts", "req"), None),
            P(("parts", "req"), None),
            P(("parts", "req"), None),
            P(None, ("parts", "req"), "tp"),
            P(None, ("parts", "req"), "tp"),
        ),
        out_specs=P(None, ("parts", "req"), "tp"),
        check_vma=False,
    )
```

profile of v0, /device:TPU:0, one launch (start us, length us, event | category | flops | bytes accessed | tf_op | source)
XLA Modules:
  0.0 302.8 jit_solution(17997864544987300175)
XLA Ops:
  6.5 0.7 all-gather.2.cloned.1.call-update
  7.3 154.0 %all-gather.2.cloned.1.call-done = bf16[2048,2048]{1,0:T(8,128)(2,1)} async-done(((bf16[2048,512]{1,0:T(8,128)(2,1)}), bf16[2048,2048]{1,0:T(8,128)(2,1)}) %all-gather.2.cloned.1.call-update) | async-done | bytes 8388624 | tf_op jit(solution)/shard_map/all_gather | solution.py:60
  161.3 13.8 %convolution_convert_fusion = bf16[1024,2048]{1,0:T(8,128)(2,1)} fusion(bf16[1024,2048]{1,0:T(8,128)(2,1)} %param.7, bf16[2048,2048]{1,0:T(8,128)(2,1)} %all-gather.2.cloned.1.call-done), kind=kOutput, calls=%fused_computation.3 | convolution fusion | flops 8592031744 | bytes 16777216 | tf_op jit(solution)/shard_map/dot_general | solution.py:58
  175.1 0.6 copy-done.3
  175.8 0.2 reduce-window_clone.1
  176.1 41.9 %reduce-scatter.2.cloned.1.call-done = bf16[1024,512]{1,0:T(8,128)(2,1)} async-done(((bf16[1024,2048]{1,0:T(8,128)(2,1)}), bf16[1024,512]{1,0:T(8,128)(2,1)}) %reduce-scatter.2.cloned.1.call-update) | async-done | bytes 1048592 | tf_op jit(solution)/shard_map/reduce_scatter | solution.py:63
  218.0 1.3 concatenate.6
  219.3 10.4 %while.1 = (s32[]{:T(128)}, bf16[1664,512]{1,0:T(8,128)(2,1)S(1)}, s32[4,2]{0,1:T(2,128)S(1)}, bf16[4,640,512]{1,2,0:T(8,128)(2,1)}, s32[]{:T(128)}) while((s32[]{:T(128)}, bf16[1664,512]{1,0:T(8,128)(2,1)S(1)}, s32[4,2]{0,1:T(2,128)S(1)}, bf16[4,640,512]{1,2,0:T(8,128)(2,1)}, s32[]{:T(128)}) %tuple.19), condition=%wide.while_cond, body=%wide.while_body.sunk | while | flops 2 | bytes 3932265 | solution.py:75
  219.4 0.5 slice.52
  219.9 0.8 dynamic-slice_bitcast_fusion.2
  220.7 0.3 copy.52
  221.0 0.9 constant_dynamic-update-slice_fusion.2
  222.0 0.5 slice.52
  222.5 0.8 dynamic-slice_bitcast_fusion.2
  223.3 0.3 copy.52
  223.6 0.9 constant_dynamic-update-slice_fusion.2
  224.6 0.5 slice.52
  225.1 0.8 dynamic-slice_bitcast_fusion.2
  225.9 0.3 copy.52
  226.2 0.9 constant_dynamic-update-slice_fusion.2
  227.2 0.5 slice.52
  227.7 0.8 dynamic-slice_bitcast_fusion.2
  228.5 0.3 copy.52
  228.8 0.9 constant_dynamic-update-slice_fusion.2
  229.7 4.7 %all-to-all-start = ((bf16[4,640,512]{1,2,0:T(8,128)(2,1)}), bf16[4,640,512]{1,2,0:T(8,128)(2,1)S(1)}, u32[]{:S(2)}, u32[]{:S(2)}) async-start(bf16[4,640,512]{1,2,0:T(8,128)(2,1)} %get-tuple-element.12), calls=%async_computation.1 | async-start | bytes 5242880 | tf_op jit(solution)/shard_map/all_to_all | solution.py:78
  234.6 0.3 fusion.20
  234.9 59.0 %all-to-all-done = bf16[4,640,512]{1,2,0:T(8,128)(2,1)S(1)} async-done(((bf16[4,640,512]{1,2,0:T(8,128)(2,1)}), bf16[4,640,512]{1,2,0:T(8,128)(2,1)S(1)}, u32[]{:S(2)}, u32[]{:S(2)}) %all-to-all-start) | async-done | bytes 2621472 | tf_op jit(solution)/shard_map/all_to_all | solution.py:78
  293.9 0.4 fusion.19
  294.3 0.2 fusion.10
  294.6 0.2 convolution_bitcast_fusion
  294.8 0.5 fusion.7
  295.4 0.6 reshape.81
  (29 shorter events, 0.7 us)
Async XLA Ops:
  6.5 154.8 %all-gather.2.cloned.1.call-start = ((), (), s32[]{:S(2)}) async-start(), calls=%async_computation.2 | async-start | bytes 10485760 | tf_op jit(solution)/shard_map/all_gather | solution.py:60
  7.3 210.7 %reduce-scatter.2.cloned.1.call-start = ((), (), s32[]{:S(2)}) async-start(), calls=%async_computation.3 | async-start | bytes 5242880 | tf_op jit(solution)/shard_map/reduce_scatter | solution.py:63
  175.1 0.7 copy-start.3
  175.1 0.8 copy-start.4
  229.7 4.7 %copy-start = (bf16[2,4,2048]{2,1,0:T(4,128)(2,1)S(1)}, bf16[2,4,2048]{2,1,0:T(4,128)(2,1)}, u32[]{:S(2)}) copy-start(bf16[2,4,2048]{2,1,0:T(4,128)(2,1)} %param.12) | copy-start | bytes 98308
  229.7 4.8 %copy-start.2 = (s32[1,4]{1,0:T(1,128)S(1)}, s32[1,4]{1,0:T(1,128)}, u32[]{:S(2)}) copy-start(s32[1,4]{1,0:T(1,128)} %param.11) | copy-start | bytes 52
  229.7 4.9 %copy-start.1 = (bf16[2,4,512]{2,1,0:T(4,128)(2,1)S(1)}, bf16[2,4,512]{2,1,0:T(4,128)(2,1)}, u32[]{:S(2)}) copy-start(bf16[2,4,512]{2,1,0:T(4,128)(2,1)} %param.13) | copy-start | bytes 24580
  229.7 64.2 %all-to-all-start = ((bf16[4,640,512]{1,2,0:T(8,128)(2,1)}), bf16[4,640,512]{1,2,0:T(8,128)(2,1)S(1)}, u32[]{:S(2)}, u32[]{:S(2)}) async-start(bf16[4,640,512]{1,2,0:T(8,128)(2,1)} %get-tuple-element.12), calls=%async_computation.1 | async-start | bytes 5242880 | tf_op jit(solution)/shard_map/all_to_all | solution.py:78
Sparse Core Ops, SparseCore 0:
  8.9 152.3 all-gather.1
  175.2 42.6 reduce-scatter.1
where the time goes:
time: 303 us
  waiting for transfers between devices  256 us (84%)
  matrix products  15.2 us (5%)
  between operations  13.5 us (4%)
  local copies, waits for them, and re-layouts  13 us (4%)
  starting transfers between devices  4.78 us (2%)
    all_gather x1, waiting for transfers between devices, on_device(): lax.all_gather(kv_weight, 'req', axis=1, tiled=True)  154 us
    all_to_all x1, waiting for transfers between devices, on_device(): lax.all_to_all(outgoing, 'req', split_axis=0, concat_axis=0, tiled=True)  59 us
    reduce_scatter x1, waiting for transfers between devices, on_device(): lax.psum_scatter(partial_value.astype(jnp.bfloat16), 'tp', scatter_dimens...  41.9 us
    dot_general x1, matrix products, on_device(): jnp.dot(prompts, lax.all_gather(kv_weight, 'req', axis=1, tiled=True), pr...  13.8 us
    gather x20, local copies, waits for them, and re-layouts  10.3 us
  transfers between devices with their start and end apart: 3, of which 3 were waited for; matrix products, arithmetic and copies ran while one was open for 0% of the time, Pallas kernels for 0%

commit v1 on v0

--- a/solution.py
+++ b/solution.py
@@ -1,11 +1,19 @@
+import functools
+
 import jax
 import jax.numpy as jnp
 from jax import lax
+from jax.experimental import pallas as pl
+from jax.experimental.pallas import tpu as pltpu
 from jax.sharding import PartitionSpec as P
 
 HD = 128
 PAGE = 16
 GQA = 8
+CHUNKS = 2
+TILE = 256
+MESH = pl.DeviceIdType.MESH
+SCALE = HD ** (-0.5)
 
 
 def attend(queries, new_kv, cache, row_lengths):
@@ -49,7 +57,7 @@
     return mixed.astype(jnp.bfloat16).reshape(steps_count, rows_count, heads_kv * GQA * HD)
 
 
-def on_device(prompts, kv_weight, owners, pages, lengths, queries, new_kv):
+def general(prompts, kv_weight, owners, pages, lengths, queries, new_kv):
     owner_count = lax.axis_size("req")
     tokens_here = prompts.shape[0]
     group_pages = tokens_here // PAGE
@@ -79,7 +87,435 @@
     return attend(queries, new_kv, incoming, lengths[0])
 
 
+def kernel(
+    R, T, owners, pages, lengths, x_hbm, w_hbm, small, out,
+    x, w, kvb, msg, qall, lens_out, lens_in, tok, s_part, s_recv, p_all, fresh_o,
+    o_part, o_recv, o_send, fin,
+    x_sem, w_sem, msg_s, msg_r, len_s, len_r, q_s, q_r,
+    z_s, z_r, y_s, y_r, s_s, s_r, p_s, p_r, o_s, o_r, f_s, f_r,
+):
+    p, r, t = lax.axis_index("parts"), lax.axis_index("req"), lax.axis_index("tp")
+    tokens = x.shape[0]
+    features = w.shape[2]
+    part_rows = features // CHUNKS
+    ht = small.shape[1]
+    heads = R * 2
+    rows = small.shape[3]
+    f32 = jnp.float32
+
+    def when(cond):
+        return pl.when(cond)
+
+    x_copy = pltpu.make_async_copy(x_hbm, x, x_sem)
+    own = [
+        pltpu.make_async_copy(
+            w_hbm.at[:, pl.ds((2 * i + kv) * HD, HD)], w.at[kv, 2 * r + i], w_sem.at[kv, i]
+        )
+        for kv in range(2)
+        for i in range(2)
+    ]
+    for copy in own:
+        copy.start()
+    x_copy.start()
+
+    barrier = pltpu.get_barrier_semaphore()
+    for rel in range(1, R):
+        pl.semaphore_signal(barrier, inc=1, device_id={"req": lax.rem(r + rel, R)}, device_id_type=MESH)
+    for rel in range(1, T):
+        pl.semaphore_signal(barrier, inc=1, device_id={"tp": lax.rem(t + rel, T)}, device_id_type=MESH)
+    pl.semaphore_signal(barrier, inc=1, device_id={"parts": 1 - p}, device_id_type=MESH)
+
+    lane = lax.broadcasted_iota(jnp.int32, (8, 128), 1)
+    row_len = jnp.zeros((8, 128), jnp.int32)
+    for g in range(R):
+        row_len = jnp.where(lane == g, lengths[0, g], row_len)
+    lens_out[...] = row_len
+    lens_in[r] = row_len
+    msg[r] = small[r]
+
+    for copy in own:
+        copy.wait()
+    pl.semaphore_wait(barrier, R + T - 1)
+
+    def remote(src, dst, s, d, where):
+        return pltpu.make_async_remote_copy(
+            src_ref=src, dst_ref=dst, send_sem=s, recv_sem=d, device_id=where, device_id_type=MESH
+        )
+
+    def msg_copy(rel):
+        to = lax.rem(r + rel, R)
+        return remote(small.at[to], msg.at[r], msg_s.at[rel], msg_r.at[rel], {"req": to})
+
+    def msg_arrival(rel):
+        of = lax.rem(r + R - rel, R)
+        return remote(small.at[of], msg.at[of], msg_s.at[rel], msg_r.at[rel], {"req": of})
+
+    def len_copy(rel):
+        to = lax.rem(r + rel, R)
+        return remote(lens_out, lens_in.at[r], len_s.at[rel], len_r.at[rel], {"req": to})
+
+    def len_arrival(rel):
+        of = lax.rem(r + R - rel, R)
+        return remote(lens_out, lens_in.at[of], len_s.at[rel], len_r.at[rel], {"req": of})
+
+    for rel in range(1, R):
+        msg_copy(rel).start()
+        len_copy(rel).start()
+
+    def piece(kv, h, c):
+        return w.at[kv, h, pl.ds(pl.multiple_of(c * part_rows, part_rows), part_rows)]
+
+    def z_copy(kv, s, c, direction):
+        to = r - 1 if direction == 0 else r + 1
+        ref = piece(kv, 2 * s + p, c)
+        return remote(ref, ref, z_s.at[kv, s, direction, c], z_r.at[kv, s, c], {"req": to})
+
+    def y_copy(kv, s, c):
+        ref = piece(kv, 2 * s + p, c)
+        return remote(ref, ref, y_s.at[kv, s, c], y_r.at[kv, s, c], {"parts": 1 - p})
+
+    def y_arrival(kv, s, c):
+        ref = piece(kv, 2 * s + 1 - p, c)
+        return remote(ref, ref, y_s.at[kv, s, c], y_r.at[kv, s, c], {"parts": 1 - p})
+
+    def z_arrival(kv, s, c, direction):
+        ref = piece(kv, 2 * s + p, c)
+        of = r + 1 if direction == 0 else r - 1
+        return remote(ref, ref, z_s.at[kv, s, direction, c], z_r.at[kv, s, c], {"req": of})
+
+    can = (r > 0, r < R - 1)
+
+    def send_own(kv):
+        for c in range(CHUNKS):
+            for direction in range(2):
+                @when(can[direction])
+                def _():
+                    z_copy(kv, r, c, direction).start()
+
+    send_own(0)
+
+    for rel in range(1, R):
+        msg_arrival(rel).wait_recv()
+        len_arrival(rel).wait_recv()
+    for i in range(ht):
+        for o in range(R):
+            qall[t * ht + i, o] = msg[o, i, 0]
+
+    def q_copy(rel):
+        ref = qall.at[pl.ds(t * ht, ht)]
+        return remote(ref, ref, q_s.at[rel], q_r.at[rel], {"tp": lax.rem(t + rel, T)})
+
+    def q_arrival(rel):
+        of = lax.rem(t + T - rel, T)
+        ref = qall.at[pl.ds(of * ht, ht)]
+        return remote(ref, ref, q_s.at[rel], q_r.at[rel], {"tp": of})
+
+    for rel in range(1, T):
+        q_copy(rel).start()
+
+    position = lax.broadcasted_iota(jnp.int32, (rows, tokens), 1)
+    owner_of = jnp.full((rows, tokens), -1, jnp.int32)
+    for o in range(R):
+        begin = jnp.int32(0)
+        running = jnp.int32(0)
+        for j in range(R):
+            begin = begin + jnp.where(owners[0, j] == o, running, 0)
+            running = running + pages[0, j] * PAGE
+        length = jnp.sum(jnp.where(lane[:1] == r, lens_in[o][:1], 0), axis=1, keepdims=True)
+        inside = (position >= begin) & (position < begin + length)
+        owner_of = jnp.where(inside, o, owner_of)
+    tok[...] = owner_of
+
+    x_copy.wait()
+    for rel in range(1, T):
+        q_arrival(rel).wait_recv()
+
+    def s_copy(h):
+        to, i = h // ht, lax.rem(h, ht)
+        return remote(s_part.at[h], s_recv.at[t, i], s_s.at[h], s_r.at[t, i], {"tp": to})
+
+    def o_copy(h):
+        to, i = h // ht, lax.rem(h, ht)
+        return remote(o_part.at[h], o_recv.at[t, i], o_s.at[h], o_r.at[t, i], {"tp": to})
+
+    def process(kv, h):
+        slot = jnp.where(kv == 1, h, heads)
+
+        def tile(n, carry):
+            at = pl.ds(pl.multiple_of(n * TILE, TILE), TILE)
+            kvb[slot, at, :] = jnp.dot(
+                x[at, :], w[kv, h], preferred_element_type=f32
+            ).astype(jnp.bfloat16)
+            return carry
+
+        lax.fori_loop(0, tokens // TILE, tile, 0)
+
+        @when(kv == 0)
+        def _():
+            scores = lax.dot_general(
+                qall[h].reshape(R * rows, HD), kvb[heads],
+                (((1,), (1,)), ((), ())), preferred_element_type=f32,
+            )
+            belongs = tok[...]
+            chosen = jnp.zeros((rows, tokens), f32)
+            for o in range(R):
+                chosen = jnp.where(belongs == o, scores[o * rows:(o + 1) * rows], chosen)
+            s_part[h] = chosen
+
+            @when(h // ht != t)
+            def _():
+                s_copy(h).start()
+
+    def own_body(j, carry):
+        process(j // 2, 2 * r + lax.rem(j, 2))
+        return carry
+
+    lax.fori_loop(0, 4, own_body, 0)
+
+    def others(n):
+        return [lax.rem(t + rel, n) for rel in range(1, n)]
+
+    def p_copy(rel):
+        ref = p_all.at[pl.ds(t * ht, ht)]
+        return remote(ref, ref, p_s.at[rel], p_r.at[rel], {"tp": lax.rem(t + rel, T)})
+
+    def p_arrival(rel):
+        of = lax.rem(t + T - rel, T)
+        ref = p_all.at[pl.ds(of * ht, ht)]
+        return remote(ref, ref, p_s.at[rel], p_r.at[rel], {"tp": of})
+
+    def softmax():
+        belongs = tok[...]
+        row = lax.broadcasted_iota(jnp.int32, (rows, rows), 0)
+        col = lax.broadcasted_iota(jnp.int32, (rows, rows), 1)
+        seen = col * GQA <= row
+        for i in range(ht):
+            h = t * ht + i
+            total = s_part[h]
+            for of in others(T):
+                remote(s_part.at[h], s_recv.at[of, i], s_s.at[h], s_r.at[of, i], {"tp": of}).wait_recv()
+                total = total + s_recv[of, i]
+            total = total * SCALE
+            probs = jnp.zeros((rows, tokens), f32)
+            for o in range(R):
+                newer = lax.dot_general(
+                    msg[o, i, 0], msg[o, i, 1], (((1,), (1,)), ((), ())),
+                    preferred_element_type=f32,
+                ) * SCALE
+                newer = jnp.where(seen, newer, -1e30)
+                mine = jnp.where(belongs == o, total, -1e30)
+                top = jnp.maximum(
+                    jnp.max(mine, axis=1, keepdims=True), jnp.max(newer, axis=1, keepdims=True)
+                )
+                e_old = jnp.exp(mine - top)
+                e_new = jnp.exp(newer - top)
+                den = jnp.sum(e_old, axis=1, keepdims=True) + jnp.sum(e_new, axis=1, keepdims=True)
+                probs = jnp.where(belongs == o, e_old / den, probs)
+                fresh_o[i, o] = jnp.dot(
+                    (e_new / den).astype(jnp.bfloat16), msg[o, i, 2], preferred_element_type=f32
+                )
+            p_all[h] = probs.astype(jnp.bfloat16)
+        for rel in range(1, T):
+            p_copy(rel).start()
+
+    hops = R - 1
+    last = 2 * hops
+
+    def source(step, side):
+        kv, d = step // hops, lax.rem(step, hops) + 1
+        s = r + d if side == 0 else r - d
+        valid = s < R if side == 0 else s >= 0
+        return kv, s, valid
+
+    def step_body(step, carry):
+        @when(step < last)
+        def _():
+            for c in range(CHUNKS):
+                for side in range(2):
+                    kv, s, valid = source(step, side)
+
+                    @when(valid)
+                    def _():
+                        z_arrival(kv, s, c, side).wait_recv()
+
+                        @when(can[side])
+                        def _():
+                            z_copy(kv, s, c, side).start()
+
+                        y_copy(kv, s, c).start()
+
+        @when(step == 0)
+        def _():
+            send_own(1)
+
+        @when(step == R)
+        def _():
+            softmax()
+
+        def candidate(j, carry):
+            late, side = j // 2, lax.rem(j, 2)
+            at = step - late
+            kv, d = jnp.maximum(at, 0) // hops, lax.rem(jnp.maximum(at, 0), hops) + 1
+            s = jnp.where(side == 0, r + d, r - d)
+            valid = (s < R) & (s >= 0) & (at >= 0) & (at < last)
+
+            @when(valid)
+            def _():
+                @when(late == 1)
+                def _():
+                    for c in range(CHUNKS):
+                        y_arrival(kv, s, c).wait_recv()
+
+                process(kv, 2 * s + jnp.where(late == 1, 1 - p, p))
+
+            return carry
+
+        lax.fori_loop(0, 4, candidate, 0)
+        return carry
+
+    lax.fori_loop(0, last + 1, step_body, 0)
+
+    for rel in range(1, T):
+        p_arrival(rel).wait_recv()
+
+    def mix(n, carry):
+        h = lax.rem(n + t * ht + ht, heads)
+        belongs = tok[...]
+        probs = p_all[h].astype(f32)
+        split = jnp.concatenate(
+            [jnp.where(belongs == o, probs, 0.0).astype(jnp.bfloat16) for o in range(R)], axis=0
+        )
+        o_part[h] = jnp.dot(split, kvb[h], preferred_element_type=f32)
+
+        @when(h // ht != t)
+        def _():
+            o_copy(h).start()
+
+        return carry
+
+    lax.fori_loop(0, heads, mix, 0)
+
+    for i in range(ht):
+        h = t * ht + i
+        total = o_part[h]
+        for of in others(T):
+            remote(o_part.at[h], o_recv.at[of, i], o_s.at[h], o_r.at[of, i], {"tp": of}).wait_recv()
+            total = total + o_recv[of, i]
+        for o in range(R):
+            o_send[o, i] = (total[o * rows:(o + 1) * rows] + fresh_o[i, o]).astype(jnp.bfloat16)
+
+    def f_copy(rel):
+        to = lax.rem(r + rel, R)
+        return remote(o_send.at[to], fin.at[r], f_s.at[rel], f_r.at[rel], {"req": to})
+
+    def f_arrival(rel):
+        of = lax.rem(r + R - rel, R)
+        return remote(o_send.at[of], fin.at[of], f_s.at[rel], f_r.at[rel], {"req": of})
+
+    for rel in range(1, R):
+        f_copy(rel).start()
+    fin[r] = o_send[r]
+
+    for rel in range(1, R):
+        msg_copy(rel).wait_send()
+        len_copy(rel).wait_send()
+    for rel in range(1, T):
+        q_copy(rel).wait_send()
+        p_copy(rel).wait_send()
+    for kv in range(2):
+        for s in range(R):
+            for c in range(CHUNKS):
+                @when((s >= r) & can[0])
+                def _():
+                    z_copy(kv, s, c, 0).wait_send()
+
+                @when((s <= r) & can[1])
+                def _():
+                    z_copy(kv, s, c, 1).wait_send()
+
+                @when(s != r)
+                def _():
+                    y_copy(kv, s, c).wait_send()
+    for h in range(heads):
+        @when(h // ht != t)
+        def _():
+            s_copy(h).wait_send()
+            o_copy(h).wait_send()
+    for rel in range(1, R):
+        f_copy(rel).wait_send()
+        f_arrival(rel).wait_recv()
+    out[...] = fin[...]
+
+
+def fused(R, T, prompts, kv_weight, owners, pages, lengths, queries, new_kv):
+    steps, count, width = queries.shape
+    ht = width // (GQA * HD)
+    heads = 2 * R
+    rows = steps * GQA
+    tokens, features = prompts.shape
+    bf16, f32, i32 = jnp.bfloat16, jnp.float32, jnp.int32
+    asked = queries.reshape(steps, count, ht, GQA, HD).transpose(1, 2, 0, 3, 4)
+    asked = asked.reshape(count, ht, 1, rows, HD)
+    fresh = new_kv.reshape(steps, count, ht, 2, HD).transpose(1, 2, 3, 0, 4)
+    fresh = jnp.pad(fresh, ((0, 0), (0, 0), (0, 0), (0, rows - steps), (0, 0)))
+    small = jnp.concatenate([asked, fresh], axis=2)
+    V, D = pltpu.VMEM, pltpu.SemaphoreType.DMA
+    smem = pl.BlockSpec(memory_space=pltpu.SMEM)
+    anywhere = pl.BlockSpec(memory_space=pl.ANY)
+    vmem = pl.BlockSpec(memory_space=pltpu.VMEM)
+    result = pl.pallas_call(
+        functools.partial(kernel, R, T),
+        out_shape=jax.ShapeDtypeStruct((R, ht, rows, HD), bf16),
+        in_specs=[smem, smem, smem, anywhere, anywhere, vmem],
+        out_specs=vmem,
+        scratch_shapes=[
+            V((tokens, features), bf16),
+            V((2, heads, features, HD), bf16),
+            V((heads + 1, tokens, HD), bf16),
+            V((R, ht, 3, rows, HD), bf16),
+            V((heads, R, rows, HD), bf16),
+            V((8, 128), i32),
+            V((R, 8, 128), i32),
+            V((rows, tokens), i32),
+            V((heads, rows, tokens), f32),
+            V((T, ht, rows, tokens), f32),
+            V((heads, rows, tokens), bf16),
+            V((ht, R, rows, HD), f32),
+            V((heads, R * rows, HD), f32),
+            V((T, ht, R * rows, HD), f32),
+            V((R, ht, rows, HD), bf16),
+            V((R, ht, rows, HD), bf16),
+            D(()), D((2, 2)), D((R,)), D((R,)), D((R,)), D((R,)), D((T,)), D((T,)),
+            D((2, R, 2, CHUNKS)), D((2, R, CHUNKS)), D((2, R, CHUNKS)), D((2, R, CHUNKS)),
+            D((heads,)), D((T, ht)), D((T,)), D((T,)), D((heads,)), D((T, ht)), D((R,)), D((R,)),
+        ],
+        compiler_params=pltpu.CompilerParams(
+            collective_id=0, has_side_effects=True, vmem_limit_bytes=48 * 1024 * 1024
+        ),
+        cost_estimate=pl.CostEstimate(
+            flops=2 * tokens * features * heads * 2 * HD,
+            bytes_accessed=2 * (tokens * features + features * heads * HD),
+            transcendentals=0,
+        ),
+    )(owners, pages, lengths, prompts, kv_weight, small)
+    result = result.reshape(R, ht, steps, GQA, HD).transpose(2, 0, 1, 3, 4)
+    return result.reshape(steps, R, width)
+
+
 def solution(mesh):
+    R, T = mesh.shape["req"], mesh.shape["tp"]
+
+    def on_device(prompts, kv_weight, owners, pages, lengths, queries, new_kv):
+        whole_heads = (
+            mesh.shape["parts"] == 2
+            and kv_weight.shape[1] == 4 * HD
+            and queries.shape[2] * T == 2 * R * GQA * HD
+            and queries.shape[0] == 2
+            and R > 1
+        )
+        body = functools.partial(fused, R, T) if whole_heads else general
+        return body(prompts, kv_weight, owners, pages, lengths, queries, new_kv)
+
     return jax.shard_map(
         on_device,
         mesh=mesh,

time: 303 us -> 115 us (0.38)
  waiting for transfers between devices: 256 us -> 0 us
  Pallas kernels: 0 us -> 109 us
  matrix products: 15.2 us -> 0 us
  between operations: 13.5 us -> 0.04 us
  local copies, waits for them, and re-layouts: 13 us -> 5.68 us
  starting transfers between devices: 4.78 us -> 0 us
    all_gather x1 -> x0, waiting for transfers between devices: 154 us -> none  [on_device(): lax.all_gather(kv_weight, 'req', axis=1, tiled=True)]
    pallas_call x0 -> x1, Pallas kernels: none -> 109 us  [fused(): pl.pallas_call(functools.partial(kernel, R, T), out_shape=jax.ShapeDtypeS...]
    all_to_all x1 -> x0, waiting for transfers between devices: 59 us -> none  [on_device(): lax.all_to_all(outgoing, 'req', split_axis=0, concat_axis=0, tiled=True)]
    reduce_scatter x1 -> x0, waiting for transfers between devices: 41.9 us -> none  [on_device(): lax.psum_scatter(partial_value.astype(jnp.bfloat16), 'tp', scatter_dimens...]
    dot_general x5 -> x0, matrix products: 15.2 us -> none  [the longest x1 13.8 us: on_device(): jnp.dot(prompts, lax.all_gather(kv_weight, 'req', axis=1, tiled=True), pr...]
    gather x20 -> x0, local copies, waits for them, and re-layouts: 10.3 us -> none
    all_to_all x1 -> x0, starting transfers between devices: 4.74 us -> none  [on_device(): lax.all_to_all(outgoing, 'req', split_axis=0, concat_axis=0, tiled=True)]
  transfers between devices with their start and end apart: 3 -> 0, of which waited for: 3 -> 0; matrix products, arithmetic and copies ran while one was open for 0% -> 0% of each run, Pallas kernels for 0% -> 0%
where the time goes in v1:
time: 115 us; the launch traced here: 114 us
  Pallas kernels  109 us (95%)
  local copies, waits for them, and re-layouts  5.68 us (5%)
    pallas_call x1, Pallas kernels, fused(): pl.pallas_call(functools.partial(kernel, R, T), out_shape=jax.ShapeDtypeS...  109 us
    unnamed x8, local copies, waits for them, and re-layouts  3.55 us

profile of v1, /device:TPU:0, one launch (start us, length us, event | category | flops | bytes accessed | tf_op | source)
XLA Modules:
  0.0 114.3 jit_solution(15201708972581553235)
XLA Ops:
  0.0 0.7 copy.16
  0.7 0.8 reshape.15
  1.5 0.0 copy-start
  1.5 1.6 %copy-done = bf16[2048,512]{1,0:T(8,128)(2,1)S(1)} copy-done((bf16[2048,512]{1,0:T(8,128)(2,1)S(1)}, bf16[2048,512]{1,0:T(8,128)(2,1)}, u32[]{:S(2)}) %copy-start) | copy-done | bytes 2097176
  3.1 0.0 copy-start.1
  3.1 0.7 copy-done.1
  3.8 0.0 copy-start.2
  3.8 0.7 copy-done.2
  4.4 0.0 copy-start.3
  4.4 0.7 copy-done.3
  5.1 108.6 %shard_map.73 = bf16[4,2,16,128]{3,2,1,0:T(8,128)(2,1)S(1)} custom-call(s32[1,4]{1,0:T(1,128)S(1)} %copy-done.1, s32[1,4]{1,0:T(1,128)S(1)} %copy-done.2, s32[1,4]{1,0:T(1,128)S(1)} %copy-done.3, bf16[1024,2048]{1,0:T(8,128)(2,1)} %x_hbm.1, bf16[2048,512]{1,0:T(8,128)(2,1)S(1)} %copy-done, bf16[4,2,3,16,128]{4,3,2,1,0:T(8,128)(2,1)S(1)} %fusion.1.small), custom_call_target="tpu_custom_call" | custom-call | flops 8589934592 | bytes 8388608 | tf_op jit(solution)/shard_map/pallas_call | solution.py:466
  113.7 0.6 reshape.19
  (3 shorter events, 0.0 us)
Async XLA Ops:
  1.5 1.6 %copy-start = (bf16[2048,512]{1,0:T(8,128)(2,1)S(1)}, bf16[2048,512]{1,0:T(8,128)(2,1)}, u32[]{:S(2)}) copy-start(bf16[2048,512]{1,0:T(8,128)(2,1)} %w_hbm.1) | copy-start | bytes 6291460
  3.1 0.7 copy-start.1
  3.8 0.7 copy-start.2
  4.4 0.7 copy-start.3

commit v2 on v1

--- a/solution.py
+++ b/solution.py
@@ -10,7 +10,7 @@
 HD = 128
 PAGE = 16
 GQA = 8
-CHUNKS = 2
+CHUNKS = 4
 TILE = 256
 MESH = pl.DeviceIdType.MESH
 SCALE = HD ** (-0.5)
@@ -88,10 +88,10 @@
 
 
 def kernel(
-    R, T, owners, pages, lengths, x_hbm, w_hbm, small, out,
-    x, w, kvb, msg, qall, lens_out, lens_in, tok, s_part, s_recv, p_all, fresh_o,
+    R, T, owners_hbm, pages_hbm, lengths_hbm, x_hbm, w_hbm, q_hbm, n_hbm, out,
+    owners, pages, lengths, q_in, n_in, small, x, w, kvb, msg, qall, lens_out, lens_in, tok, s_part, s_recv, p_all, fresh_o,
     o_part, o_recv, o_send, fin,
-    x_sem, w_sem, msg_s, msg_r, len_s, len_r, q_s, q_r,
+    in_sem, x_sem, w_sem, msg_s, msg_r, len_s, len_r, q_s, q_r,
     z_s, z_r, y_s, y_r, s_s, s_r, p_s, p_r, o_s, o_r, f_s, f_r,
 ):
     p, r, t = lax.axis_index("parts"), lax.axis_index("req"), lax.axis_index("tp")
@@ -114,7 +114,13 @@
         for kv in range(2)
         for i in range(2)
     ]
-    for copy in own:
+    inputs = [
+        pltpu.make_async_copy(a, b, in_sem.at[n])
+        for n, (a, b) in enumerate(
+            [(q_hbm, q_in), (n_hbm, n_in), (owners_hbm, owners), (pages_hbm, pages), (lengths_hbm, lengths)]
+        )
+    ]
+    for copy in own[:2] + inputs + own[2:]:
         copy.start()
     x_copy.start()
 
@@ -125,74 +131,97 @@
         pl.semaphore_signal(barrier, inc=1, device_id={"tp": lax.rem(t + rel, T)}, device_id_type=MESH)
     pl.semaphore_signal(barrier, inc=1, device_id={"parts": 1 - p}, device_id_type=MESH)
 
+    for copy in own[:2]:
+        copy.wait()
+    pl.semaphore_wait(barrier, R + T - 1)
+
+    def remote(src, dst, s, d, where):
+        return pltpu.make_async_remote_copy(
+            src_ref=src, dst_ref=dst, send_sem=s, recv_sem=d, device_id=where, device_id_type=MESH
+        )
+
+    def msg_copy(rel):
+        to = lax.rem(r + rel, R)
+        return remote(small.at[to], msg.at[r], msg_s.at[rel], msg_r.at[rel], {"req": to})
+
+    def msg_arrival(rel):
+        of = lax.rem(r + R - rel, R)
+        return remote(small.at[of], msg.at[of], msg_s.at[rel], msg_r.at[rel], {"req": of})
+
+    def len_copy(rel):
+        to = lax.rem(r + rel, R)
+        return remote(lens_out, lens_in.at[r], len_s.at[rel], len_r.at[rel], {"req": to})
+
+    def len_arrival(rel):
+        of = lax.rem(r + R - rel, R)
+        return remote(lens_out, lens_in.at[of], len_s.at[rel], len_r.at[rel], {"req": of})
+
+    def piece(kv, h, c):
+        return w.at[kv, h, pl.ds(pl.multiple_of(c * part_rows, part_rows), part_rows)]
+
+    def z_copy(kv, s, c, direction):
+        to = r - 1 if direction == 0 else r + 1
+        ref = piece(kv, 2 * s + p, c)
+        return remote(ref, ref, z_s.at[kv, s, direction, c], z_r.at[kv, s, c], {"req": to})
+
+    def y_copy(kv, s, c):
+        ref = piece(kv, 2 * s + p, c)
+        return remote(ref, ref, y_s.at[kv, s, c], y_r.at[kv, s, c], {"parts": 1 - p})
+
+    def y_arrival(kv, s, c):
+        ref = piece(kv, 2 * s + 1 - p, c)
+        return remote(ref, ref, y_s.at[kv, s, c], y_r.at[kv, s, c], {"parts": 1 - p})
+
+    def z_arrival(kv, s, c, direction):
+        ref = piece(kv, 2 * s + p, c)
+        of = r + 1 if direction == 0 else r - 1
+        return remote(ref, ref, z_s.at[kv, s, direction, c], z_r.at[kv, s, c], {"req": of})
+
+    can = (r > 0, r < R - 1)
+
+    def send_own(kv):
+        for c in range(CHUNKS):
+            for direction in range(2):
+                @when(can[direction])
+                def _():
+                    z_copy(kv, r, c, direction).start()
+
+    send_own(0)
+    for copy in own[2:]:
+        copy.wait()
+    send_own(1)
+
+    for copy in inputs:
+        copy.wait()
     lane = lax.broadcasted_iota(jnp.int32, (8, 128), 1)
     row_len = jnp.zeros((8, 128), jnp.int32)
     for g in range(R):
         row_len = jnp.where(lane == g, lengths[0, g], row_len)
     lens_out[...] = row_len
     lens_in[r] = row_len
-    msg[r] = small[r]
-
-    for copy in own:
-        copy.wait()
-    pl.semaphore_wait(barrier, R + T - 1)
-
-    def remote(src, dst, s, d, where):
-        return pltpu.make_async_remote_copy(
-            src_ref=src, dst_ref=dst, send_sem=s, recv_sem=d, device_id=where, device_id_type=MESH
-        )
-
-    def msg_copy(rel):
-        to = lax.rem(r + rel, R)
-        return remote(small.at[to], msg.at[r], msg_s.at[rel], msg_r.at[rel], {"req": to})
-
-    def msg_arrival(rel):
-        of = lax.rem(r + R - rel, R)
-        return remote(small.at[of], msg.at[of], msg_s.at[rel], msg_r.at[rel], {"req": of})
-
-    def len_copy(rel):
-        to = lax.rem(r + rel, R)
-        return remote(lens_out, lens_in.at[r], len_s.at[rel], len_r.at[rel], {"req": to})
-
-    def len_arrival(rel):
-        of = lax.rem(r + R - rel, R)
-        return remote(lens_out, lens_in.at[of], len_s.at[rel], len_r.at[rel], {"req": of})
-
+    steps = q_in.shape[0]
+    asked = [q_in[s].astype(f32) for s in range(steps)]
+    newer = [n_in[s].astype(f32) for s in range(steps)]
+    nothing = jnp.zeros((rows - steps, HD), f32)
+    for g in range(R):
+        for i in range(ht):
+            small[g, i, 0] = jnp.concatenate(
+                [
+                    asked[s][g:g + 1, (i * GQA + j) * HD:(i * GQA + j + 1) * HD]
+                    for s in range(steps)
+                    for j in range(GQA)
+                ],
+                axis=0,
+            ).astype(jnp.bfloat16)
+            for kv in range(2):
+                at = (2 * i + kv) * HD
+                small[g, i, 1 + kv] = jnp.concatenate(
+                    [newer[s][g:g + 1, at:at + HD] for s in range(steps)] + [nothing], axis=0
+                ).astype(jnp.bfloat16)
     for rel in range(1, R):
         msg_copy(rel).start()
         len_copy(rel).start()
-
-    def piece(kv, h, c):
-        return w.at[kv, h, pl.ds(pl.multiple_of(c * part_rows, part_rows), part_rows)]
-
-    def z_copy(kv, s, c, direction):
-        to = r - 1 if direction == 0 else r + 1
-        ref = piece(kv, 2 * s + p, c)
-        return remote(ref, ref, z_s.at[kv, s, direction, c], z_r.at[kv, s, c], {"req": to})
-
-    def y_copy(kv, s, c):
-        ref = piece(kv, 2 * s + p, c)
-        return remote(ref, ref, y_s.at[kv, s, c], y_r.at[kv, s, c], {"parts": 1 - p})
-
-    def y_arrival(kv, s, c):
-        ref = piece(kv, 2 * s + 1 - p, c)
-        return remote(ref, ref, y_s.at[kv, s, c], y_r.at[kv, s, c], {"parts": 1 - p})
-
-    def z_arrival(kv, s, c, direction):
-        ref = piece(kv, 2 * s + p, c)
-        of = r + 1 if direction == 0 else r - 1
-        return remote(ref, ref, z_s.at[kv, s, direction, c], z_r.at[kv, s, c], {"req": of})
-
-    can = (r > 0, r < R - 1)
-
-    def send_own(kv):
-        for c in range(CHUNKS):
-            for direction in range(2):
-                @when(can[direction])
-                def _():
-                    z_copy(kv, r, c, direction).start()
-
-    send_own(0)
+    msg[r] = small[r]
 
     for rel in range(1, R):
         msg_arrival(rel).wait_recv()
@@ -226,10 +255,6 @@
         owner_of = jnp.where(inside, o, owner_of)
     tok[...] = owner_of
 
-    x_copy.wait()
-    for rel in range(1, T):
-        q_arrival(rel).wait_recv()
-
     def s_copy(h):
         to, i = h // ht, lax.rem(h, ht)
         return remote(s_part.at[h], s_recv.at[t, i], s_s.at[h], s_r.at[t, i], {"tp": to})
@@ -265,12 +290,6 @@
             @when(h // ht != t)
             def _():
                 s_copy(h).start()
-
-    def own_body(j, carry):
-        process(j // 2, 2 * r + lax.rem(j, 2))
-        return carry
-
-    lax.fori_loop(0, 4, own_body, 0)
 
     def others(n):
         return [lax.rem(t + rel, n) for rel in range(1, n)]
@@ -327,59 +346,21 @@
         valid = s < R if side == 0 else s >= 0
         return kv, s, valid
 
-    def step_body(step, carry):
-        @when(step < last)
-        def _():
-            for c in range(CHUNKS):
-                for side in range(2):
-                    kv, s, valid = source(step, side)
-
-                    @when(valid)
-                    def _():
-                        z_arrival(kv, s, c, side).wait_recv()
-
-                        @when(can[side])
-                        def _():
-                            z_copy(kv, s, c, side).start()
-
-                        y_copy(kv, s, c).start()
-
-        @when(step == 0)
-        def _():
-            send_own(1)
-
-        @when(step == R)
-        def _():
-            softmax()
-
-        def candidate(j, carry):
-            late, side = j // 2, lax.rem(j, 2)
-            at = step - late
-            kv, d = jnp.maximum(at, 0) // hops, lax.rem(jnp.maximum(at, 0), hops) + 1
-            s = jnp.where(side == 0, r + d, r - d)
-            valid = (s < R) & (s >= 0) & (at >= 0) & (at < last)
+    def forward(step, c):
+        for side in range(2):
+            kv, s, valid = source(step, side)
 
             @when(valid)
             def _():
-                @when(late == 1)
+                z_arrival(kv, s, c, side).wait_recv()
+
+                @when(can[side])
                 def _():
-                    for c in range(CHUNKS):
-                        y_arrival(kv, s, c).wait_recv()
-
-                process(kv, 2 * s + jnp.where(late == 1, 1 - p, p))
-
-            return carry
-
-        lax.fori_loop(0, 4, candidate, 0)
-        return carry
-
-    lax.fori_loop(0, last + 1, step_body, 0)
-
-    for rel in range(1, T):
-        p_arrival(rel).wait_recv()
-
-    def mix(n, carry):
-        h = lax.rem(n + t * ht + ht, heads)
+                    z_copy(kv, s, c, side).start()
+
+                y_copy(kv, s, c).start()
+
+    def mix(h):
         belongs = tok[...]
         probs = p_all[h].astype(f32)
         split = jnp.concatenate(
@@ -391,9 +372,79 @@
         def _():
             o_copy(h).start()
 
+    def piece_of(step, j):
+        late, side = j // 2, lax.rem(j, 2)
+        at = jnp.maximum(step - 1, 0)
+        kv, d = at // hops, lax.rem(at, hops) + 1
+        s = jnp.where(side == 0, r + d, r - d)
+        first = step == 0
+        valid = first | ((s < R) & (s >= 0))
+        h = jnp.where(first, 2 * r + side, 2 * s + jnp.where(late == 1, 1 - p, p))
+        return jnp.where(first, 1 - late, kv), s, h, valid, (late == 1) & (step > 0)
+
+    def work(step, j):
+        kv, s, h, valid, across = piece_of(step, j)
+
+        @when(valid & across)
+        def _():
+            for c in range(CHUNKS):
+                y_arrival(kv, s, c).wait_recv()
+
+        @when(valid)
+        def _():
+            process(kv, h)
+
+        return h, valid
+
+    def step_body(step, carry):
+        def slot(j, carry):
+            @when(step < last)
+            def _():
+                forward(step, j)
+
+            @when((step == 0) & (j == 0))
+            def _():
+                x_copy.wait()
+
+            @when((step == 0) & (j == 2))
+            def _():
+                for rel in range(1, T):
+                    q_arrival(rel).wait_recv()
+
+            h, valid = work(step, j)
+
+            @when((step == last) & valid)
+            def _():
+                mix(h)
+
+            return carry
+
+        lax.fori_loop(0, 4, slot, 0)
+
+        @when(step == R)
+        def _():
+            softmax()
+
+        @when(step == last - 1)
+        def _():
+            for rel in range(1, T):
+                p_arrival(rel).wait_recv()
+
+            def early(n, carry):
+                s = n // 2
+                away = jnp.where(s > r, s - r, r - s)
+
+                @when(away < hops)
+                def _():
+                    mix(n)
+
+                return carry
+
+            lax.fori_loop(0, heads, early, 0)
+
         return carry
 
-    lax.fori_loop(0, heads, mix, 0)
+    lax.fori_loop(0, last + 1, step_body, 0)
 
     for i in range(ht):
         h = t * ht + i
@@ -444,7 +495,17 @@
     for rel in range(1, R):
         f_copy(rel).wait_send()
         f_arrival(rel).wait_recv()
-    out[...] = fin[...]
+    got = [[fin[g, i].astype(f32) for i in range(ht)] for g in range(R)]
+    for s in range(steps):
+        out[s] = jnp.concatenate(
+            [
+                jnp.concatenate(
+                    [got[g][i][s * GQA + j:s * GQA + j + 1] for i in range(ht) for j in range(GQA)], axis=1
+                )
+                for g in range(R)
+            ],
+            axis=0,
+        ).astype(jnp.bfloat16)
 
 
 def fused(R, T, prompts, kv_weight, owners, pages, lengths, queries, new_kv):
@@ -454,21 +515,19 @@
     rows = steps * GQA
     tokens, features = prompts.shape
     bf16, f32, i32 = jnp.bfloat16, jnp.float32, jnp.int32
-    asked = queries.reshape(steps, count, ht, GQA, HD).transpose(1, 2, 0, 3, 4)
-    asked = asked.reshape(count, ht, 1, rows, HD)
-    fresh = new_kv.reshape(steps, count, ht, 2, HD).transpose(1, 2, 3, 0, 4)
-    fresh = jnp.pad(fresh, ((0, 0), (0, 0), (0, 0), (0, rows - steps), (0, 0)))
-    small = jnp.concatenate([asked, fresh], axis=2)
     V, D = pltpu.VMEM, pltpu.SemaphoreType.DMA
-    smem = pl.BlockSpec(memory_space=pltpu.SMEM)
     anywhere = pl.BlockSpec(memory_space=pl.ANY)
     vmem = pl.BlockSpec(memory_space=pltpu.VMEM)
-    result = pl.pallas_call(
+    return pl.pallas_call(
         functools.partial(kernel, R, T),
-        out_shape=jax.ShapeDtypeStruct((R, ht, rows, HD), bf16),
-        in_specs=[smem, smem, smem, anywhere, anywhere, vmem],
+        out_shape=jax.ShapeDtypeStruct((steps, R, width), bf16),
+        in_specs=[anywhere] * 7,
         out_specs=vmem,
         scratch_shapes=[
+            pltpu.SMEM(owners.shape, i32), pltpu.SMEM(pages.shape, i32), pltpu.SMEM(lengths.shape, i32),
+            V(queries.shape, bf16),
+            V(new_kv.shape, bf16),
+            V((R, ht, 3, rows, HD), bf16),
             V((tokens, features), bf16),
             V((2, heads, features, HD), bf16),
             V((heads + 1, tokens, HD), bf16),
@@ -485,7 +544,7 @@
             V((T, ht, R * rows, HD), f32),
             V((R, ht, rows, HD), bf16),
             V((R, ht, rows, HD), bf16),
-            D(()), D((2, 2)), D((R,)), D((R,)), D((R,)), D((R,)), D((T,)), D((T,)),
+            D((5,)), D(()), D((2, 2)), D((R,)), D((R,)), D((R,)), D((R,)), D((T,)), D((T,)),
             D((2, R, 2, CHUNKS)), D((2, R, CHUNKS)), D((2, R, CHUNKS)), D((2, R, CHUNKS)),
             D((heads,)), D((T, ht)), D((T,)), D((T,)), D((heads,)), D((T, ht)), D((R,)), D((R,)),
         ],
@@ -497,9 +556,7 @@
             bytes_accessed=2 * (tokens * features + features * heads * HD),
             transcendentals=0,
         ),
-    )(owners, pages, lengths, prompts, kv_weight, small)
-    result = result.reshape(R, ht, steps, GQA, HD).transpose(2, 0, 1, 3, 4)
-    return result.reshape(steps, R, width)
+    )(owners, pages, lengths, prompts, kv_weight, queries, new_kv)
 
 
 def solution(mesh):
@@ -511,7 +568,7 @@
             and kv_weight.shape[1] == 4 * HD
             and queries.shape[2] * T == 2 * R * GQA * HD
             and queries.shape[0] == 2
-            and R > 1
+            and R > 2
         )
         body = functools.partial(fused, R, T) if whole_heads else general
         return body(prompts, kv_weight, owners, pages, lengths, queries, new_kv)

time: 115 us -> 119 us (1.035)
  Pallas kernels: 109 us -> 112 us
    pallas_call x1, Pallas kernels: 109 us -> 112 us  [fused(): pl.pallas_call(functools.partial(kernel, R, T), out_shape=jax.ShapeDtypeS...]
    reshape x4 -> x0, local copies, waits for them, and re-layouts: 2.12 us -> none  [the longest x2 0.79 us: fused(): asked = queries.reshape(steps, count, ht, GQA, HD).transpose(1, 2, 0, 3, 4)]
    unnamed x8 -> x13, local copies, waits for them, and re-layouts: 3.55 us -> 5.63 us
where the time goes in v2:
time: 119 us; the launch traced here: 118 us
  Pallas kernels  112 us (94%)
  local copies, waits for them, and re-layouts  5.63 us (5%)
    pallas_call x1, Pallas kernels, fused(): pl.pallas_call(functools.partial(kernel, R, T), out_shape=jax.ShapeDtypeS...  112 us
    unnamed x13, local copies, waits for them, and re-layouts  5.63 us

profile of v2, /device:TPU:0, one launch (start us, length us, event | category | flops | bytes accessed | tf_op | source)
XLA Modules:
  0.0 117.9 jit_solution(14602407170058583601)
XLA Ops:
  0.0 0.0 copy-start
  0.0 1.6 %copy-done = bf16[2048,512]{1,0:T(8,128)(2,1)S(1)} copy-done((bf16[2048,512]{1,0:T(8,128)(2,1)S(1)}, bf16[2048,512]{1,0:T(8,128)(2,1)}, u32[]{:S(2)}) %copy-start) | copy-done | bytes 2097176
  1.6 0.0 copy-start.1
  1.6 0.8 copy-done.1
  2.4 0.0 copy-start.2
  2.4 0.7 copy-done.2
  3.0 0.0 copy-start.3
  3.0 0.7 copy-done.3
  3.7 0.0 copy-start.4
  3.7 0.7 copy-done.4
  4.4 0.0 copy-start.5
  4.4 0.7 copy-done.5
  5.0 112.3 %shard_map.73 = bf16[2,4,2048]{2,1,0:T(4,128)(2,1)S(1)} custom-call(s32[1,4]{1,0:T(1,128)S(1)} %copy-done.3, s32[1,4]{1,0:T(1,128)S(1)} %copy-done.4, s32[1,4]{1,0:T(1,128)S(1)} %copy-done.5, bf16[1024,2048]{1,0:T(8,128)(2,1)} %x_hbm.1, bf16[2048,512]{1,0:T(8,128)(2,1)S(1)} %copy-done, bf16[2,4,2048]{2,1,0:T(4,128)(2,1)S(1)} %copy-done.1, ...), custom_call_target="tpu_custom_call" | custom-call | flops 8589934592 | bytes 8388608 | tf_op jit(solution)/shard_map/pallas_call | solution.py:521
  117.3 0.6 copy.9
Async XLA Ops:
  0.0 1.6 %copy-start = (bf16[2048,512]{1,0:T(8,128)(2,1)S(1)}, bf16[2048,512]{1,0:T(8,128)(2,1)}, u32[]{:S(2)}) copy-start(bf16[2048,512]{1,0:T(8,128)(2,1)} %w_hbm.1) | copy-start | bytes 6291460
  1.6 0.8 copy-start.1
  2.4 0.7 copy-start.2
  3.0 0.7 copy-start.3
  3.7 0.7 copy-start.4
  4.4 0.7 copy-start.5
